TPU v7x, 256 devices: a whole 4x4x8 slice. The times are simulated.
256 devices in a mesh: pool: 32 (over x_hi, z, core), tp: 8 (over x_lo, y).
Axes of the slice: x: 4 (x_hi: 2, x_lo: 2; x = x_hi * 2 + x_lo), y: 4, z: 8, core: 2. Of those that a mesh axis runs over, the one named last changes fastest.
Arguments:
- queries: bfloat16 [32768, 8192], P('pool', 'tp'), may hold values from -10 to 10
- keys: bfloat16 [32768, 1024], P('pool', 'tp'), may hold values from -6 to 6
- values: bfloat16 [32768, 1024], P('pool', 'tp'), may hold values from -6 to 6
- start_pages: int32 [32], P('pool'), may hold values from 0 to 255
- owners: int32 [32, 16, 1], P('pool'), may hold values from 0 to 31; in each aligned block of 16 rows (0 to 15, 16 to 31, ..., all dimensions but the last counted through in order) at most 2 rows name the same one
Outputs:
- mixed: bfloat16 [32768, 8192], P('pool', 'tp')
- store: bfloat16 [2048, 64, 2, 1024], P(('pool', 'tp'))
Inputs may be any that keep to these rules, and one draw needn't show every extreme that they name: `owners`: in each group at most 2 pages name the same owner, and some group has exactly 2 pages with one owner.
All inputs are finite; a program needn't handle non-finite values.
Results may differ from a plain program's by a relative error of at most 0.011.
Values may be sent and summed in bfloat16 or wider, within the bound.
A program may use at most 128 MiB of HBM per device.

v0:
```python
import math

import jax
import jax.numpy as jnp
from jax import lax
from jax.sharding import PartitionSpec as P

HD = 128
PAGE = 64
CAP = 2


ROPE_THETA = 1000000.0


def rotate(tensor, position):
    half_dim = tensor.shape[-1] // 2
    inverse = ROPE_THETA ** (-(jnp.arange(half_dim, dtype=jnp.float32) * 2.0) / (2.0 * half_dim))
    angles = position[:, None] * inverse[None, :]
    cosine = jnp.concatenate([jnp.cos(angles), jnp.cos(angles)], axis=-1)
    sine = jnp.concatenate([jnp.sin(angles), jnp.sin(angles)], axis=-1)
    first = tensor[..., :half_dim]
    second = tensor[..., half_dim:]
    turned = jnp.concatenate([-second, first], axis=-1)
    extended = (tensor.shape[0],) + (1,) * (tensor.ndim - 2) + (tensor.shape[-1],)
    return tensor * cosine.reshape(extended) + turned * sine.reshape(extended)


def attend(query_rot, key_rot, value_heads):
    length = query_rot.shape[0]
    block = min(512, length)
    scale = 1.0 / math.sqrt(query_rot.shape[-1])
    results = []
    for block_index in range(length // block):
        finish = (block_index + 1) * block
        query_block = query_rot[block_index * block : finish]
        scores = (
            jnp.einsum(
                "qkgd,skd->kgqs", query_block, key_rot[:finish], preferred_element_type=jnp.float32
            )
            * scale
        )
        query_pos = block_index * block + jnp.arange(block)
        key_pos = jnp.arange(finish)
        allowed = key_pos[None, :] <= query_pos[:, None]
        scores = jnp.where(allowed, scores, jnp.float32(-1e30))
        highest = jnp.max(scores, axis=-1, keepdims=True)
        weights = jnp.exp(scores - highest)
        total = jnp.sum(weights, axis=-1, keepdims=True)
        probs = (weights / total).astype(jnp.bfloat16)
        output = jnp.einsum(
            "kgqs,skd->qkgd", probs, value_heads[:finish], preferred_element_type=jnp.float32
        )
        results.append(output.astype(jnp.bfloat16).reshape(block, -1))
    return jnp.concatenate(results, axis=0)


def on_device(queries, keys, values, start_pages, owners):
    tokens_here = queries.shape[0]
    kv_local = keys.shape[1] // HD
    group_size = queries.shape[1] // (HD * kv_local)
    position = (PAGE * start_pages[0] + jnp.arange(tokens_here)).astype(jnp.float32)
    query_rot = rotate(
        queries.reshape(tokens_here, kv_local, group_size, HD).astype(jnp.float32), position
    ).astype(jnp.bfloat16)
    key_rot = rotate(keys.reshape(tokens_here, kv_local, HD).astype(jnp.float32), position).astype(
        jnp.bfloat16
    )
    value_heads = values.reshape(tokens_here, kv_local, HD)
    mixed = attend(query_rot, key_rot, value_heads)
    pool_size = lax.axis_size("pool")
    page_count = tokens_here // PAGE
    owner_ids = owners[0, :, 0]
    earlier = jnp.arange(page_count)[None, :] < jnp.arange(page_count)[:, None]
    same_owner = owner_ids[:, None] == owner_ids[None, :]
    rank = jnp.sum(jnp.logical_and(same_owner, earlier), axis=1)
    slot_ids = owner_ids * CAP + rank
    select = (jnp.arange(pool_size * CAP, dtype=jnp.int32)[:, None] == slot_ids[None, :]).astype(
        jnp.bfloat16
    )
    pieces = jnp.stack([key_rot.reshape(tokens_here, kv_local * HD), values], axis=1)
    pieces = pieces.reshape(page_count, PAGE, 2, kv_local * HD)
    outgoing = jnp.einsum(
        "sp,pqcw->sqcw", select, pieces, preferred_element_type=jnp.float32
    ).astype(jnp.bfloat16)
    outgoing = outgoing.reshape(pool_size, CAP, PAGE, 2, kv_local * HD)
    landed = lax.all_to_all(outgoing, "pool", split_axis=0, concat_axis=0, tiled=True)
    arrived = lax.all_to_all(landed, "tp", split_axis=0, concat_axis=4, tiled=True)
    store = arrived.reshape(-1, PAGE, 2, arrived.shape[-1])
    return (mixed, store)


def solution(mesh):
    return jax.shard_map(
        on_device,
        mesh=mesh,
        in_specs=(
            P("pool", "tp"),
            P("pool", "tp"),
            P("pool", "tp"),
            P("pool"),
            P("pool", None, None),
        ),
        out_specs=(P("pool", "tp"), P(("pool", "tp"), None, None, None)),
        check_vma=False,
    )
```

profile of v0, /device:TPU:32, one launch (start us, length us, event | category | flops | bytes accessed | tf_op | source)
XLA Modules:
  0.0 112.9 jit_solution(13296853482998145211)
XLA Ops:
  0.6 0.0 copy-start.2
  0.7 0.0 copy-start.4
  0.7 1.0 convert_bitcast_fusion
  1.7 0.2 fusion.21
  2.6 1.9 %multiply_cosine_fusion = (f32[1024,64]{1,0:T(8,128)S(1)}, f32[1024,64]{1,0:T(8,128)S(1)}) fusion(f32[64]{0:T(128)S(1)} %multiply_power_fusion, f32[1024]{0:T(1024)S(1)} %add_convert_fusion), kind=kLoop, calls=%fused_computation.30 | loop fusion | flops 65536 | bytes 528640 | tf_op jit(solution)/shard_map/cos | solution.py:20
  4.5 2.2 %fusion.20 = (bf16[1024,128]{1,0:T(8,128)(2,1)S(1)}, f32[1024,128]{1,0:T(8,128)S(1)}, f32[1024,128]{1,0:T(8,128)}) fusion(bf16[1024,128]{1,0:T(8,128)(2,1)} %param.6, f32[1024,64]{1,0:T(8,128)S(1)} %get-tuple-element.8, f32[1024,64]{1,0:T(8,128)S(1)} %get-tuple-element.7, f32[1024,64]{1,0:T(8,128)S(1)} %get-tuple-element.10, f32[1024,64]{1,0:T(8,128)S(1)} %get-tuple-element.9), kind=kLoop, calls=%fused_computation.34 | loop fusion | flops 1048576 | bytes 2621440 | tf_op jit(solution)/shard_map/convert_element_type | solution.py:66
  6.7 0.2 copy.52
  6.9 0.0 copy-done.2
  6.9 0.2 copy.53
  7.1 0.0 copy-done.4
  7.1 0.2 convert_reduce_fusion
  7.3 0.8 convolution_convert_fusion
  8.1 3.5 %copy.54 = bf16[32,2,64,2,128]{4,1,3,2,0:T(2,128)(2,1)} copy(bf16[32,2,64,2,128]{4,1,0,3,2:T(2,128)(2,1)S(1)} %bitcast.107) | data formatting | bytes 4194304 | tf_op jit(solution)/shard_map/reshape | solution.py:86
  11.6 11.2 %all-to-all-start = ((bf16[32,2,64,2,128]{4,1,3,2,0:T(2,128)(2,1)}), bf16[32,2,64,2,128]{4,1,3,2,0:T(2,128)(2,1)}, u32[]{:S(2)}, u32[]{:S(2)}) async-start(bf16[32,2,64,2,128]{4,1,3,2,0:T(2,128)(2,1)} %copy.54), calls=%async_computation | async-start | bytes 4194304 | tf_op jit(solution)/shard_map/all_to_all | solution.py:87
  22.9 0.1 iota_compare_fusion.1
  23.0 2.9 %copy.42 = bf16[1024,1024]{0,1:T(8,128)(2,1)S(1)} copy(bf16[1024,1024]{1,0:T(8,128)(2,1)} %param.5) | data formatting | bytes 4194304 | tf_op args[0]
  25.8 2.8 %copy.43 = f32[1024,1,8,128]{3,0,2,1:T(8,128)} copy(bf16[1024,1,8,128]{0,3,2,1:T(8,128)(2,1)S(1)} %bitcast.105) | data formatting | bytes 6291456 | tf_op jit(solution)/shard_map/convert_element_type | solution.py:64
  28.7 0.0 copy-start
  28.7 0.0 copy-start.1
  28.7 5.0 %slice_negate_fusion = (f32[1024,1,8,64]{3,0,2,1:T(8,128)S(1)}, f32[1024,1,8,64]{3,0,2,1:T(8,128)S(1)}) fusion(f32[1024,1,8,128]{3,0,2,1:T(8,128)} %copy.43), kind=kLoop, calls=%fused_computation.12 | loop fusion | flops 524288 | bytes 8388608 | tf_op jit(solution)/shard_map/neg | solution.py:24
  33.7 0.0 copy-done
  33.7 0.0 copy-done.1
  33.7 1.3 %fusion.7 = bf16[1024,1,8,128]{3,0,2,1:T(8,128)(2,1)S(1)} fusion(f32[1024,1,8,64]{3,0,2,1:T(8,128)S(1)} %get-tuple-element.3, f32[1024,1,8,64]{3,0,2,1:T(8,128)S(1)} %get-tuple-element.2, f32[1024,1,8,128]{3,0,2,1:T(8,128)S(1)} %copy-done, f32[1024,128]{1,0:T(8,128)S(1)} %copy-done.1, f32[1024,128]{1,0:T(8,128)S(1)} %get-tuple-element.5), kind=kLoop, calls=%fused_computation.15 | loop fusion | flops 5242880 | bytes 11534336 | tf_op jit(solution)/shard_map/convert_element_type | solution.py:65
  35.1 1.5 %fusion.5 = (f32[8,512]{1,0:T(8,128)S(1)}, f32[512,512,8]{1,0,2:T(8,128)S(1)}) fusion(pred[512,512]{0,1:T(8,128)(4,1)S(1)} %iota_compare_fusion.1, bf16[1024,1,8,128]{3,0,2,1:T(8,128)(2,1)S(1)} %fusion.7, bf16[1024,128]{1,0:T(8,128)(2,1)S(1)} %get-tuple-element.4), kind=kOutput, calls=%fused_computation.11 | convolution fusion | flops 543158272 | bytes 9846784 | tf_op jit(solution)/shard_map/qkgd,skd->kgqs/dot_general | solution.py:38
  36.6 1.8 %fusion.4 = f32[8,512]{1,0:T(8,128)S(1)} fusion(f32[512,512,8]{1,0,2:T(8,128)S(1)} %get-tuple-element.14, f32[8,512]{1,0:T(8,128)S(1)} %get-tuple-element.13, pred[512,512]{0,1:T(8,128)(4,1)S(1)} %iota_compare_fusion.1), kind=kLoop, calls=%fused_computation.10 | loop fusion | flops 8384512 | bytes 8683520 | tf_op jit(solution)/shard_map/reduce_sum | solution.py:49
  38.3 3.5 %fusion.11 = bf16[8,512,128]{1,2,0:T(8,128)(2,1)} fusion(f32[8,512]{1,0:T(8,128)S(1)} %fusion.4, f32[8,512]{1,0:T(8,128)S(1)} %get-tuple-element.13, f32[512,512,8]{1,0,2:T(8,128)S(1)} %get-tuple-element.14, pred[512,512]{0,1:T(8,128)(4,1)S(1)} %iota_compare_fusion.1, bf16[1024,128]{1,0:T(8,128)(2,1)S(1)} %copy-done.2), kind=kOutput, calls=%fused_computation.22 | convolution fusion | flops 547880960 | bytes 9863168 | tf_op jit(solution)/shard_map/kgqs,skd->qkgd/dot_general | solution.py:51
  41.8 2.3 %copy.50 = bf16[512,1024]{1,0:T(8,128)(2,1)} copy(bf16[512,1024]{0,1:T(8,128)(2,1)} %bitcast.109) | data formatting | bytes 2097152 | tf_op jit(solution)/shard_map/reshape | solution.py:54
  44.1 0.4 iota_compare_fusion
  44.5 7.3 %fusion.1 = (f32[8,512]{1,0:T(8,128)S(1)}, f32[1024,512,8]{1,0,2:T(8,128)}) fusion(pred[512,1024]{0,1:T(8,128)(4,1)S(1)} %iota_compare_fusion, bf16[1024,1,8,128]{3,0,2,1:T(8,128)(2,1)S(1)} %fusion.7, bf16[1024,128]{1,0:T(8,128)(2,1)S(1)} %get-tuple-element.4), kind=kOutput, calls=%fused_computation.4 | convolution fusion | flops 1086320640 | bytes 18628608 | tf_op jit(solution)/shard_map/qkgd,skd->kgqs/dot_general | solution.py:38
  51.8 9.2 %fusion = f32[8,512]{1,0:T(8,128)S(1)} fusion(f32[1024,512,8]{1,0,2:T(8,128)} %get-tuple-element.12, f32[8,512]{1,0:T(8,128)S(1)} %get-tuple-element.11, pred[512,1024]{0,1:T(8,128)(4,1)S(1)} %iota_compare_fusion), kind=kLoop, calls=%fused_computation.3 | loop fusion | flops 16773120 | bytes 17334272 | tf_op jit(solution)/shard_map/reduce_sum | solution.py:49
  61.0 0.0 copy-start.3
  61.0 14.9 %all-to-all-done = bf16[32,2,64,2,128]{4,1,3,2,0:T(2,128)(2,1)} async-done(((bf16[32,2,64,2,128]{4,1,3,2,0:T(2,128)(2,1)}), bf16[32,2,64,2,128]{4,1,3,2,0:T(2,128)(2,1)}, u32[]{:S(2)}, u32[]{:S(2)}) %all-to-all-start) | async-done | bytes 2097184 | tf_op jit(solution)/shard_map/all_to_all | solution.py:87
  75.9 4.5 %all-to-all-start.1 = ((bf16[32,2,64,2,128]{4,1,3,2,0:T(2,128)(2,1)}), bf16[32,2,64,2,128]{4,1,3,2,0:T(2,128)(2,1)S(1)}, u32[]{:S(2)}, u32[]{:S(2)}) async-start(bf16[32,2,64,2,128]{4,1,3,2,0:T(2,128)(2,1)} %all-to-all-done), calls=%async_computation.1 | async-start | bytes 4194304 | tf_op jit(solution)/shard_map/all_to_all | solution.py:88
  80.4 0.0 copy-done.3
  80.4 9.3 %fusion.14 = bf16[8,512,128]{1,2,0:T(8,128)(2,1)} fusion(f32[8,512]{1,0:T(8,128)S(1)} %fusion, f32[8,512]{1,0:T(8,128)S(1)} %get-tuple-element.11, f32[1024,512,8]{1,0,2:T(8,128)} %get-tuple-element.12, pred[512,1024]{0,1:T(8,128)(4,1)S(1)} %iota_compare_fusion, bf16[1024,128]{1,0:T(8,128)(2,1)S(1)} %copy-done.3), kind=kOutput, calls=%fused_computation.23 | convolution fusion | flops 1095237632 | bytes 18644992 | tf_op jit(solution)/shard_map/kgqs,skd->qkgd/dot_general | solution.py:51
  89.7 1.5 %copy.51 = bf16[512,1024]{1,0:T(8,128)(2,1)S(1)} copy(bf16[512,1024]{0,1:T(8,128)(2,1)} %bitcast.110) | data formatting | bytes 2097152 | tf_op jit(solution)/shard_map/reshape | solution.py:54
  91.2 2.7 %pad_maximum_fusion = bf16[1024,1024]{1,0:T(8,128)(2,1)} fusion(bf16[512,1024]{1,0:T(8,128)(2,1)S(1)} %copy.51, bf16[512,1024]{1,0:T(8,128)(2,1)} %copy.50), kind=kLoop, calls=%fused_computation.19 | loop fusion | flops 4194304 | bytes 4194304 | tf_op jit(solution)/shard_map/concatenate | solution.py:55
  93.9 12.3 %all-to-all-done.1 = bf16[32,2,64,2,128]{4,1,3,2,0:T(2,128)(2,1)S(1)} async-done(((bf16[32,2,64,2,128]{4,1,3,2,0:T(2,128)(2,1)}), bf16[32,2,64,2,128]{4,1,3,2,0:T(2,128)(2,1)S(1)}, u32[]{:S(2)}, u32[]{:S(2)}) %all-to-all-start.1) | async-done | bytes 2097184 | tf_op jit(solution)/shard_map/all_to_all | solution.py:88
  106.2 2.7 %copy.55 = bf16[4,2,64,2,8,128]{5,4,3,2,1,0:T(8,128)(2,1)} copy(bf16[4,2,64,2,8,128]{5,1,3,2,0,4:T(2,128)(2,1)S(1)} %bitcast.106) | data formatting | bytes 4194304 | tf_op jit(solution)/shard_map/all_to_all | solution.py:88
  108.9 4.0 %reshape.187 = bf16[8,64,2,1024]{3,2,1,0:T(2,128)(2,1)} reshape(bf16[4,2,64,2,8,128]{5,4,3,2,1,0:T(8,128)(2,1)} %copy.55) | data formatting | bytes 4194304 | tf_op jit(solution)/shard_map/reshape | solution.py:89
  (4 shorter events, 0.0 us)
Async XLA Ops:
  0.6 6.2 %copy-start.2 = (bf16[1024,128]{1,0:T(8,128)(2,1)S(1)}, bf16[1024,128]{1,0:T(8,128)(2,1)}, u32[]{:S(2)}) copy-start(bf16[1024,128]{1,0:T(8,128)(2,1)} %param.7) | copy-start | bytes 786436
  0.7 6.4 %copy-start.4 = (s32[1,16,1]{1,2,0:T(1,128)S(1)}, s32[1,16,1]{1,2,0:T(1,128)}, u32[]{:S(2)}) copy-start(s32[1,16,1]{1,2,0:T(1,128)} %param.9) | copy-start | bytes 196
  11.6 64.3 %all-to-all-start = ((bf16[32,2,64,2,128]{4,1,3,2,0:T(2,128)(2,1)}), bf16[32,2,64,2,128]{4,1,3,2,0:T(2,128)(2,1)}, u32[]{:S(2)}, u32[]{:S(2)}) async-start(bf16[32,2,64,2,128]{4,1,3,2,0:T(2,128)(2,1)} %copy.54), calls=%async_computation | async-start | bytes 4194304 | tf_op jit(solution)/shard_map/all_to_all | solution.py:87
  28.7 5.0 %copy-start = (f32[1024,1,8,128]{3,0,2,1:T(8,128)S(1)}, f32[1024,1,8,128]{3,0,2,1:T(8,128)}, u32[]{:S(2)}) copy-start(f32[1024,1,8,128]{3,0,2,1:T(8,128)} %copy.43) | copy-start | bytes 12582916
  28.7 5.0 %copy-start.1 = (f32[1024,128]{1,0:T(8,128)S(1)}, f32[1024,128]{1,0:T(8,128)}, u32[]{:S(2)}) copy-start(f32[1024,128]{1,0:T(8,128)} %get-tuple-element.6) | copy-start | bytes 1572868
  61.0 19.4 %copy-start.3 = (bf16[1024,128]{1,0:T(8,128)(2,1)S(1)}, bf16[1024,128]{1,0:T(8,128)(2,1)}, u32[]{:S(2)}) copy-start(bf16[1024,128]{1,0:T(8,128)(2,1)} %param.7) | copy-start | bytes 786436
  75.9 30.3 %all-to-all-start.1 = ((bf16[32,2,64,2,128]{4,1,3,2,0:T(2,128)(2,1)}), bf16[32,2,64,2,128]{4,1,3,2,0:T(2,128)(2,1)S(1)}, u32[]{:S(2)}, u32[]{:S(2)}) async-start(bf16[32,2,64,2,128]{4,1,3,2,0:T(2,128)(2,1)} %all-to-all-done), calls=%async_computation.1 | async-start | bytes 4194304 | tf_op jit(solution)/shard_map/all_to_all | solution.py:88
where the time goes:
time: 113 us
  waiting for transfers between devices  27.3 us (24%)
  other arithmetic  26 us (23%)
  matrix products  22.4 us (20%)
  local copies, waits for them, and re-layouts  20 us (18%)
  starting transfers between devices  15.7 us (14%)
  between operations  1.45 us (1%)
    all_to_all x1, waiting for transfers between devices, on_device(): lax.all_to_all(outgoing, 'pool', split_axis=0, concat_axis=0, tiled=True)  14.9 us
    dot_general x2, matrix products, attend(): jnp.einsum('kgqs,skd->qkgd', probs, value_heads[:finish], preferred_eleme...  12.8 us
    all_to_all x1, waiting for transfers between devices, on_device(): lax.all_to_all(landed, 'tp', split_axis=0, concat_axis=4, tiled=True)  12.3 us
    all_to_all x1, starting transfers between devices, on_device(): lax.all_to_all(outgoing, 'pool', split_axis=0, concat_axis=0, tiled=True)  11.2 us
    reduce_sum x2, other arithmetic, attend(): total = jnp.sum(weights, axis=-1, keepdims=True)  10.9 us
    dot_general x2, matrix products, attend(): jnp.einsum('qkgd,skd->kgqs', query_block, key_rot[:finish], preferred_ele...  8.79 us
    neg x1, other arithmetic, rotate(): turned = jnp.concatenate([-second, first], axis=-1)  4.99 us
    all_to_all x1, starting transfers between devices, on_device(): lax.all_to_all(landed, 'tp', split_axis=0, concat_axis=4, tiled=True)  4.5 us
  transfers between devices with their start and end apart: 2, of which 2 were waited for; matrix products, arithmetic and copies ran while one was open for 46% of the time, Pallas kernels for 0%

commit v1 on v0

v1 whole, which is shorter than its diff:
```python
import functools
import math

import jax
import jax.numpy as jnp
import numpy as np
from jax import lax
from jax.experimental import pallas as pl
from jax.experimental.pallas import tpu as pltpu
from jax.sharding import PartitionSpec as P

HD = 128
PAGE = 64
ROPE_THETA = 1000000.0
MESH = pl.DeviceIdType.MESH
NZ = 8
NP = 16
T = 1024
NH = 8
C = 4
AHEAD = 2
LATE = 4
R = 2 * PAGE // C
BQ = 256
NQ = T // BQ
F32 = jnp.float32
BF16 = jnp.bfloat16


def dev(xh, z, c, xl, y):
    return (xh * 16 + z * 2 + c, xl * 4 + y)


def dot_t(a, b):
    return lax.dot_general(a, b, (((1,), (1,)), ((), ())), preferred_element_type=F32)


def main_kernel(inv_ref, start_ref, owners_ref, q_hbm, k_hbm, v_hbm, mixed_hbm, land, *scratch):
    (qbuf, kbuf, vbuf, mbuf, cos_t, sin_t, krot, vext, tbl, tbl_in, tbl_s,
     xs, d3o, d4o, in_sem, tl_sem, t_send, t_recv, r_send, r_recv, d3_send, d3_recv,
     d4_send, d4_recv, p_send, p_recv, x_send, l_recv, out_sem) = scratch[:29]
    blocks = scratch[29:]
    raw = blocks[0:C]
    ra = (blocks[C:2 * C], blocks[2 * C:3 * C])
    rb = (blocks[3 * C:4 * C], blocks[4 * C:5 * C])

    p_idx, t_idx = lax.axis_index("pool"), lax.axis_index("tp")
    xh, z, c = p_idx // 16, (p_idx // 2) % 8, p_idx % 2
    xl, y = t_idx // 4, t_idx % 4
    edge = 1 - (xl - xh) * (xl - xh)
    is_edge = xl == xh
    other = 1 - xh
    pxh, pxl = xh + edge * (1 - 2 * xh), xl + edge * (1 - 2 * xl)

    k_in = pltpu.make_async_copy(k_hbm, kbuf, in_sem.at[0])
    v_in = pltpu.make_async_copy(v_hbm, vbuf, in_sem.at[1])
    q_in = pltpu.make_async_copy(q_hbm, qbuf, in_sem.at[2])
    k_in.start()
    v_in.start()
    q_in.start()

    bar = pltpu.get_barrier_semaphore()

    def greet(*place):
        pl.semaphore_signal(bar, inc=1, device_id=dev(*place), device_id_type=MESH)

    for n in (1, 7, 2, 6):
        greet(xh, (z + n) % NZ, c, xl, y)

    @pl.when(is_edge)
    def _():
        for n in (0, 1, 7, 2, 6):
            greet(pxh, (z + n) % NZ, c, pxl, y)

    for half in range(2):
        xhd, xld = half + edge * (xh - half), xh + edge * (half - xh)
        for y2 in range(4):
            for c2 in range(2):
                here = is_edge & (half == xl) & (y2 == y) & (c2 == c)

                @pl.when(jnp.logical_not(here))
                def _():
                    greet(xhd, z, c2, xld, y2)

    own = [owners_ref[q] for q in range(NP)]
    lane = lax.broadcasted_iota(jnp.int32, (8, 128), 1)
    table = jnp.full((8, 128), -1, jnp.int32)
    for q in range(NP):
        rank = jnp.int32(0)
        for e in range(q):
            rank = rank + jnp.where(own[e] == own[q], 1, 0)
        table = jnp.where(lane == own[q] * 2 + rank, q, table)
    tbl[...] = table

    inv = inv_ref[...]
    base = start_ref[0] * PAGE
    page_pos = (base + PAGE * lax.broadcasted_iota(jnp.int32, (NP, HD), 0)).astype(F32)
    in_pos = lax.broadcasted_iota(jnp.int32, (PAGE, HD), 0).astype(F32)
    ang_p = page_pos * inv
    ang_i = in_pos * inv
    cos_p, sin_p, cos_i, sin_i = jnp.cos(ang_p), jnp.sin(ang_p), jnp.cos(ang_i), jnp.sin(ang_i)
    sign = jnp.where(lax.broadcasted_iota(jnp.int32, (PAGE, HD), 1) < HD // 2, -1.0, 1.0).astype(F32)
    row = lax.broadcasted_iota(jnp.int32, (2 * PAGE, 2 * PAGE), 0)
    col = lax.broadcasted_iota(jnp.int32, (2 * PAGE, 2 * PAGE), 1)
    weave = (col == (row // 2) + PAGE * (row % 2)).astype(BF16)
    k_in.wait()
    v_in.wait()
    for q in range(NP):
        rows = slice(q * PAGE, (q + 1) * PAGE)
        cos_q = cos_p[q:q + 1] * cos_i - sin_p[q:q + 1] * sin_i
        sin_q = (sin_p[q:q + 1] * cos_i + cos_p[q:q + 1] * sin_i) * sign
        cos_t[rows] = cos_q
        sin_t[rows] = sin_q
        k = kbuf[rows].astype(F32)
        kr = (k * cos_q + pltpu.roll(k, HD // 2, 1) * sin_q).astype(BF16)
        krot[rows] = kr
        v = vbuf[rows]
        both = jnp.dot(weave, jnp.concatenate([kr, v], axis=0), preferred_element_type=F32).astype(BF16)
        for k_ in range(C):
            raw[k_][q] = both[k_ * R:(k_ + 1) * R]
        vext[rows, 0:HD] = v
        vext[rows, HD:] = jnp.ones((PAGE, HD), BF16)

    pl.semaphore_wait(bar, 20 + 4 * edge)

    t_copies = []
    for e, n in enumerate((1, 7, 2, 6)):
        t_copies.append(pltpu.make_async_remote_copy(
            src_ref=tbl, dst_ref=tbl_in.at[e], send_sem=t_send.at[e], recv_sem=t_recv.at[e],
            device_id=dev(xh, (z + n) % NZ, c, xl, y), device_id_type=MESH))
    own_tbl = pltpu.make_async_copy(tbl, tbl_s.at[0], tl_sem.at[0])

    def raw_copy(stage, k, d):
        return pltpu.make_async_remote_copy(
            src_ref=raw[k] if stage == 0 else ra[d][k], dst_ref=ra[d][k] if stage == 0 else rb[d][k],
            send_sem=r_send.at[stage, k, d], recv_sem=r_recv.at[stage, k, d],
            device_id=dev(xh, (z + (1, 7)[d]) % NZ, c, xl, y), device_id_type=MESH)

    def d3_copy(k, d, half):
        swap = edge * (xh if half == 0 else 1 - xh)
        to = half + swap * (xh - half)
        return pltpu.make_async_remote_copy(
            src_ref=d3o.at[d, k, half], dst_ref=xs.at[k, (5, 3)[d], to],
            send_sem=d3_send.at[k, d, half], recv_sem=d3_recv.at[k, d, to],
            device_id=dev(xh + swap * (1 - 2 * xh), (z + (1, 7)[d]) % NZ, c, xl + swap * (1 - 2 * xl), y),
            device_id_type=MESH)

    def d4_copy(k, d):
        swap = 0 if d == 0 else edge
        to = xh if d == 0 else other + edge * (xh - other)
        return pltpu.make_async_remote_copy(
            src_ref=d4o.at[d, k], dst_ref=xs.at[k, 4, to],
            send_sem=d4_send.at[k, d], recv_sem=d4_recv.at[k, to],
            device_id=dev(xh + swap * (1 - 2 * xh), (z + (2, 6)[d]) % NZ, c, xl + swap * (1 - 2 * xl), y),
            device_id_type=MESH)

    def pass_copy(k, dz):
        return pltpu.make_async_remote_copy(
            src_ref=xs.at[k, dz, 2], dst_ref=xs.at[k, dz, xh],
            send_sem=p_send.at[k, dz], recv_sem=p_recv.at[k, dz],
            device_id=dev(pxh, z, c, pxl, y), device_id_type=MESH)

    def to_owner(k, dz, second):
        zs = (z + dz) % NZ
        y2 = zs // 2
        if second:
            half, xhd, xld = other, other + edge * (xh - other), xh + edge * (other - xh)
            hxl = xl + edge * (1 - 2 * xl)
        else:
            half, xhd, xld, hxl = xh, xh, xh, xl
        for c2 in range(2):
            src = xs.at[k, dz, half, c2]
            at = (((zs % 2) * 2 + c) * 8 + hxl * 4 + y) * 2
            dst = land.at[pl.ds(at, 2), pl.ds(k * R, R)]

            def remote():
                pltpu.make_async_remote_copy(
                    src_ref=src, dst_ref=dst, send_sem=x_send, recv_sem=l_recv,
                    device_id=dev(xhd, z, c2, xld, y2), device_id_type=MESH).start()

            if second:
                remote()
            else:
                here = is_edge & (y2 == y) & (c2 == c)

                @pl.when(here)
                def _():
                    pltpu.make_async_copy(src, dst, l_recv).start()

                pl.when(jnp.logical_not(here))(remote)

    def pick(ref, which, slot):
        idx = tbl_s[which, 0, slot]
        page = ref[jnp.maximum(idx, 0)]
        return jnp.where(idx >= 0, page, jnp.zeros_like(page))

    def extract(ref, which, k, dz):
        for half in range(2):
            swap = edge * (xh if half == 0 else 1 - xh)
            to = half + swap * (2 - half)
            for c2 in range(2):
                for r in range(2):
                    xs[k, dz, to, c2, r] = pick(ref, which, half * 32 + z * 4 + c2 * 2 + r)

        @pl.when(is_edge)
        def _():
            pass_copy(k, dz).start()

        to_owner(k, dz, False)

    def passed(k, dz):
        @pl.when(is_edge)
        def _():
            pass_copy(k, dz).wait_recv()

        to_owner(k, dz, True)

    def ev_tables():
        for e, cp in enumerate(t_copies):
            cp.wait()
            pltpu.make_async_copy(tbl_in.at[e], tbl_s.at[e + 1], tl_sem.at[e + 1]).start()
        for e in range(4):
            pltpu.make_async_copy(tbl_in.at[e], tbl_s.at[e + 1], tl_sem.at[e + 1]).wait()

    def ev_own(k):
        extract(raw[k], 0, k, 0)

    def ev_one(k):
        for d in range(2):
            raw_copy(0, k, d).wait_recv()
            raw_copy(1, k, d).start()
        if k + AHEAD < C:
            for d in range(2):
                raw_copy(0, k + AHEAD, d).start()
        for d in range(2):
            extract(ra[d][k], 1 + d, k, (7, 1)[d])

    def ev_two(k):
        for d in range(2):
            raw_copy(1, k, d).wait_recv()
            n3, n4 = ((1, 2), (7, 6))[d]
            half4 = xh if d == 0 else other
            for c2 in range(2):
                for r in range(2):
                    d4o[d, k, c2, r] = pick(rb[d][k], 3 + d, half4 * 32 + ((z + n4) % NZ) * 4 + c2 * 2 + r)
            d4_copy(k, d).start()
            for half in range(2):
                for c2 in range(2):
                    for r in range(2):
                        d3o[d, k, half, c2, r] = pick(rb[d][k], 3 + d, half * 32 + ((z + n3) % NZ) * 4 + c2 * 2 + r)
                d3_copy(k, d, half).start()
        for d in range(2):
            extract(rb[d][k], 3 + d, k, (6, 2)[d])

    def ev_pass1(k):
        for dz in (0, 7, 1):
            passed(k, dz)

    def ev_far(k):
        for dz in (6, 2):
            passed(k, dz)
        for d in range(2):
            for half in range(2):
                d3_copy_in(k, d, half)
            to_owner(k, (5, 3)[d], False)
            to_owner(k, (5, 3)[d], True)
        for half in range(2):
            d4_copy_in(k, half)
        to_owner(k, 4, False)
        to_owner(k, 4, True)

    def d3_copy_in(k, d, half):
        landed = xs.at[k, (5, 3)[d], half]
        pltpu.make_async_copy(landed, landed, d3_recv.at[k, d, half]).wait()

    def d4_copy_in(k, half):
        landed = xs.at[k, 4, half]
        pltpu.make_async_copy(landed, landed, d4_recv.at[k, half]).wait()

    scale = math.log2(math.e) / math.sqrt(HD)

    def attend(h, i):
        rows = slice(i * BQ, (i + 1) * BQ)
        cols = pl.ds(pl.multiple_of(h * HD, HD), HD)
        q = qbuf[rows, cols].astype(F32)
        qr = (q * cos_t[rows] + pltpu.roll(q, HD // 2, 1) * sin_t[rows]).astype(BF16)
        s_d = dot_t(qr, krot[rows])
        keep = (lax.broadcasted_iota(jnp.int32, (BQ, BQ), 1) <= lax.broadcasted_iota(jnp.int32, (BQ, BQ), 0))
        s_d = jnp.where(keep, s_d, -1e30)
        top = jnp.max(s_d, axis=1, keepdims=True)
        if i > 0:
            s_f = dot_t(qr, krot[0:i * BQ])
            top = jnp.maximum(top, jnp.max(s_f, axis=1, keepdims=True))
        w_d = jnp.exp2((s_d - top) * scale).astype(BF16)
        out = jnp.dot(w_d, vext[rows], preferred_element_type=F32)
        if i > 0:
            w_f = jnp.exp2((s_f - top) * scale).astype(BF16)
            out = out + jnp.dot(w_f, vext[0:i * BQ], preferred_element_type=F32)
        mbuf[rows, cols] = (out[:, 0:HD] / out[:, HD:]).astype(BF16)

    own_tbl.start()
    for k in range(AHEAD):
        for d in range(2):
            raw_copy(0, k, d).start()
        if k == 0:
            for cp in t_copies:
                cp.start()
    own_tbl.wait()
    q_in.wait()

    events = [functools.partial(ev_own, 0), ev_tables]
    for r in range(C + 2):
        if r < C:
            events.append(functools.partial(ev_one, r))
            if r + 1 < C:
                events.append(functools.partial(ev_own, r + 1))
        if 0 <= r - 1 < C:
            events.append(functools.partial(ev_two, r - 1))
            events.append(functools.partial(ev_pass1, r - 1))
        if 0 <= r - 2 < C:
            events.append(functools.partial(ev_far, r - 2))
    units = NH * NQ
    at_step = {}
    for n, e in enumerate(events[:-LATE]):
        at_step.setdefault(n * units // (len(events) - LATE), []).append(e)

    def unit(s, carry):
        for n, es in at_step.items():
            @pl.when(s == n)
            def _():
                for e in es:
                    e()
        h, i = s // NQ, s % NQ
        for j in range(NQ):
            @pl.when(i == j)
            def _():
                attend(h, j)
        return carry

    lax.fori_loop(0, units, unit, 0)
    out = pltpu.make_async_copy(mbuf, mixed_hbm, out_sem)
    out.start()
    for e in events[-LATE:]:
        e()
    out.wait()
    for k in range(C):
        for d in range(2):
            raw_copy(0, k, d).wait_send()
            raw_copy(1, k, d).wait_send()
            d4_copy(k, d).wait_send()
            for half in range(2):
                d3_copy(k, d, half).wait_send()

        @pl.when(is_edge)
        def _():
            for dz in (0, 7, 1, 6, 2):
                pass_copy(k, dz).wait_send()
    whole = land.at[pl.ds(0, 60)]
    pltpu.make_async_copy(whole, whole, x_send).wait()

    @pl.when(jnp.logical_not(is_edge))
    def _():
        rest = land.at[pl.ds(60, 4)]
        pltpu.make_async_copy(rest, rest, x_send).wait()

    pltpu.make_async_copy(land, land, l_recv).wait()


def layout_kernel(land, mixed_in, store, mixed, lbuf, mbuf, sem, msem):
    parts = 4
    rows = T // parts
    ins, outs = [], []
    for g in range(4):
        ins.append(pltpu.make_async_copy(land.at[pl.ds(g * 16, 16)], lbuf.at[pl.ds(g * 16, 16)], sem.at[0, g]))
        ins.append(pltpu.make_async_copy(
            mixed_in.at[pl.ds(g * rows, rows)], mbuf.at[pl.ds(g * rows, rows)], msem.at[0, g]))
    for cp in ins:
        cp.start()
    for g in range(4):
        ins[2 * g].wait()
        for h in range(8):
            for r in range(2):
                outs.append(pltpu.make_async_copy(
                    lbuf.at[(g * 8 + h) * 2 + r], store.at[g * 2 + r, :, :, pl.ds(h * HD, HD)],
                    sem.at[1 + h * 2 + r, g]))
                outs[-1].start()
        ins[2 * g + 1].wait()
        outs.append(pltpu.make_async_copy(
            mbuf.at[pl.ds(g * rows, rows)], mixed.at[pl.ds(g * rows, rows)], msem.at[1, g]))
        outs[-1].start()
    for cp in outs:
        cp.wait()


def on_device(queries, keys, values, start_pages, owners):
    half = HD // 2
    inv = ROPE_THETA ** (-(np.arange(half, dtype=np.float64) * 2.0) / HD)
    inv = jnp.asarray(np.concatenate([inv, inv]).astype(np.float32).reshape(1, HD))
    anys = pl.BlockSpec(memory_space=pl.ANY)
    smem = pl.BlockSpec(memory_space=pltpu.SMEM)
    vm = lambda *s: pltpu.VMEM(s, BF16)
    dma = lambda *s: pltpu.SemaphoreType.DMA(s) if s else pltpu.SemaphoreType.DMA
    blocks = [vm(NP, R, HD)] * (5 * C)
    mixed, land = pl.pallas_call(
        main_kernel,
        out_shape=(jax.ShapeDtypeStruct((T, NH * HD), BF16), jax.ShapeDtypeStruct((64, 2 * PAGE, HD), BF16)),
        in_specs=[pl.BlockSpec(memory_space=pltpu.VMEM), smem, smem, anys, anys, anys],
        out_specs=(anys, anys),
        scratch_shapes=[
            vm(T, NH * HD), vm(T, HD), vm(T, HD), vm(T, NH * HD),
            pltpu.VMEM((T, HD), F32), pltpu.VMEM((T, HD), F32), vm(T, HD), vm(T, 2 * HD),
            pltpu.VMEM((8, 128), jnp.int32), pltpu.VMEM((4, 8, 128), jnp.int32), pltpu.SMEM((5, 8, 128), jnp.int32),
            vm(C, NZ, 3, 2, 2, R, HD), vm(2, C, 2, 2, 2, R, HD), vm(2, C, 2, 2, R, HD),
            dma(3), dma(5),
            dma(4), dma(4),
            dma(2, C, 2), dma(2, C, 2), dma(C, 2, 2), dma(C, 2, 2), dma(C, 2), dma(C, 2), dma(C, NZ), dma(C, NZ),
            dma(), dma(), dma(),
        ] + blocks,
        compiler_params=pltpu.CompilerParams(
            collective_id=0, has_side_effects=True, vmem_limit_bytes=56 << 20),
    )(inv, start_pages, owners.reshape(NP), queries, keys, values)
    store, mixed = pl.pallas_call(
        layout_kernel,
        out_shape=(jax.ShapeDtypeStruct((8, PAGE, 2, 8 * HD), BF16), jax.ShapeDtypeStruct((T, NH * HD), BF16)),
        in_specs=[anys, anys],
        out_specs=(anys, anys),
        scratch_shapes=[vm(64, PAGE, 2, HD), vm(T, NH * HD), dma(17, 4), dma(2, 4)],
        compiler_params=pltpu.CompilerParams(vmem_limit_bytes=24 << 20),
    )(land.reshape(64, PAGE, 2, HD), mixed)
    return (mixed, store)


def solution(mesh):
    return jax.shard_map(
        on_device,
        mesh=mesh,
        in_specs=(
            P("pool", "tp"),
            P("pool", "tp"),
            P("pool", "tp"),
            P("pool"),
            P("pool", None, None),
        ),
        out_specs=(P("pool", "tp"), P(("pool", "tp"), None, None, None)),
        check_vma=False,
    )
```

time: 113 us -> 71.3 us (0.63)
  the two profiles are of different devices: /device:TPU:32 before, /device:TPU:19 now
where the time goes in v1:
time: 71.3 us; the launch traced here: 71.1 us
  Pallas kernels  66.6 us (93%)
  local copies, waits for them, and re-layouts  3.17 us (4%)
  between operations  1.29 us (2%)
    pallas_call x1, Pallas kernels, on_device(): pl.pallas_call(main_kernel, out_shape=(jax.ShapeDtypeStruct((T, NH * HD),...  63.7 us
    unnamed x4, local copies, waits for them, and re-layouts  3.17 us
    pallas_call x1, Pallas kernels, on_device(): pl.pallas_call(layout_kernel, out_shape=(jax.ShapeDtypeStruct((8, PAGE, 2...  2.94 us

profile of v1, /device:TPU:19, one launch (start us, length us, event | category | flops | bytes accessed | tf_op | source)
XLA Modules:
  0.0 71.1 jit_solution(7161869058331969529)
XLA Ops:
  1.3 63.7 %shard_map.77 = (bf16[1024,1024]{1,0:T(8,128)(2,1)}, bf16[64,128,128]{2,1,0:T(8,128)(2,1)}) custom-call(f32[1,128]{1,0:T(1,128)} %constant.2.clone.inv_ref, s32[1]{0:T(128)S(6)} %copy.8.start_ref, s32[16]{0:T(128)} %bitcast.3, bf16[1024,1024]{1,0:T(8,128)(2,1)} %q_hbm.1, bf16[1024,128]{1,0:T(8,128)(2,1)} %k_hbm.1, bf16[1024,128]{1,0:T(8,128)(2,1)} %v_hbm.1), custom_call_target="tpu_custom_call" | custom-call | tf_op jit(solution)/shard_map/pallas_call | solution.py:404
  64.9 0.0 copy-start
  65.0 1.6 %copy-done = bf16[1024,1024]{1,0:T(8,128)(2,1)S(1)} copy-done((bf16[1024,1024]{1,0:T(8,128)(2,1)S(1)}, bf16[1024,1024]{1,0:T(8,128)(2,1)}, u32[]{:S(2)}) %copy-start) | copy-done | bytes 2097176
  66.5 0.0 copy-start.1
  66.5 1.6 %copy-done.1 = bf16[64,128,128]{2,1,0:T(8,128)(2,1)S(1)} copy-done((bf16[64,128,128]{2,1,0:T(8,128)(2,1)S(1)}, bf16[64,128,128]{2,1,0:T(8,128)(2,1)}, u32[]{:S(2)}) %copy-start.1) | copy-done | bytes 2097176
  68.1 2.9 %shard_map.78 = (bf16[8,64,2,1024]{3,2,1,0:T(2,128)(2,1)}, bf16[1024,1024]{1,0:T(8,128)(2,1)}) custom-call(bf16[64,64,2,128]{3,2,1,0:T(2,128)(2,1)S(1)} %bitcast.2, bf16[1024,1024]{1,0:T(8,128)(2,1)S(1)} %copy-done), custom_call_target="tpu_custom_call" | custom-call | tf_op jit(solution)/shard_map/pallas_call | solution.py:422
Async XLA Ops:
  64.9 1.6 %copy-start = (bf16[1024,1024]{1,0:T(8,128)(2,1)S(1)}, bf16[1024,1024]{1,0:T(8,128)(2,1)}, u32[]{:S(2)}) copy-start(bf16[1024,1024]{1,0:T(8,128)(2,1)} %get-tuple-element.7.mixed_in) | copy-start | bytes 6291460
  66.5 1.6 %copy-start.1 = (bf16[64,128,128]{2,1,0:T(8,128)(2,1)S(1)}, bf16[64,128,128]{2,1,0:T(8,128)(2,1)}, u32[]{:S(2)}) copy-start(bf16[64,128,128]{2,1,0:T(8,128)(2,1)} %get-tuple-element.6) | copy-start | bytes 6291460

commit v2 on v1

--- a/solution.py
+++ b/solution.py
@@ -17,11 +17,11 @@
 NP = 16
 T = 1024
 NH = 8
-C = 4
-AHEAD = 2
-LATE = 4
+C = 8
+AHEAD = 3
 R = 2 * PAGE // C
 BQ = 256
+HG = 4
 NQ = T // BQ
 F32 = jnp.float32
 BF16 = jnp.bfloat16
@@ -57,7 +57,6 @@
     q_in = pltpu.make_async_copy(q_hbm, qbuf, in_sem.at[2])
     k_in.start()
     v_in.start()
-    q_in.start()
 
     bar = pltpu.get_barrier_semaphore()
 
@@ -105,6 +104,7 @@
     weave = (col == (row // 2) + PAGE * (row % 2)).astype(BF16)
     k_in.wait()
     v_in.wait()
+    q_in.start()
     for q in range(NP):
         rows = slice(q * PAGE, (q + 1) * PAGE)
         cos_q = cos_p[q:q + 1] * cos_i - sin_p[q:q + 1] * sin_i
@@ -232,6 +232,8 @@
         if k + AHEAD < C:
             for d in range(2):
                 raw_copy(0, k + AHEAD, d).start()
+
+    def ev_one_out(k):
         for d in range(2):
             extract(ra[d][k], 1 + d, k, (7, 1)[d])
 
@@ -249,6 +251,8 @@
                     for r in range(2):
                         d3o[d, k, half, c2, r] = pick(rb[d][k], 3 + d, half * 32 + ((z + n3) % NZ) * 4 + c2 * 2 + r)
                 d3_copy(k, d, half).start()
+
+    def ev_two_out(k):
         for d in range(2):
             extract(rb[d][k], 3 + d, k, (6, 2)[d])
 
@@ -281,22 +285,22 @@
 
     def attend(h, i):
         rows = slice(i * BQ, (i + 1) * BQ)
-        cols = pl.ds(pl.multiple_of(h * HD, HD), HD)
-        q = qbuf[rows, cols].astype(F32)
-        qr = (q * cos_t[rows] + pltpu.roll(q, HD // 2, 1) * sin_t[rows]).astype(BF16)
-        s_d = dot_t(qr, krot[rows])
         keep = (lax.broadcasted_iota(jnp.int32, (BQ, BQ), 1) <= lax.broadcasted_iota(jnp.int32, (BQ, BQ), 0))
-        s_d = jnp.where(keep, s_d, -1e30)
-        top = jnp.max(s_d, axis=1, keepdims=True)
-        if i > 0:
-            s_f = dot_t(qr, krot[0:i * BQ])
-            top = jnp.maximum(top, jnp.max(s_f, axis=1, keepdims=True))
-        w_d = jnp.exp2((s_d - top) * scale).astype(BF16)
-        out = jnp.dot(w_d, vext[rows], preferred_element_type=F32)
-        if i > 0:
-            w_f = jnp.exp2((s_f - top) * scale).astype(BF16)
-            out = out + jnp.dot(w_f, vext[0:i * BQ], preferred_element_type=F32)
-        mbuf[rows, cols] = (out[:, 0:HD] / out[:, HD:]).astype(BF16)
+        for g in range(HG):
+            cols = pl.ds(pl.multiple_of((h * HG + g) * HD, HD), HD)
+            q = qbuf[rows, cols].astype(F32)
+            qr = (q * cos_t[rows] + pltpu.roll(q, HD // 2, 1) * sin_t[rows]).astype(BF16)
+            s_d = jnp.where(keep, dot_t(qr, krot[rows]), -1e30)
+            top = jnp.max(s_d, axis=1, keepdims=True)
+            if i > 0:
+                s_f = dot_t(qr, krot[0:i * BQ])
+                top = jnp.maximum(top, jnp.max(s_f, axis=1, keepdims=True))
+            w_d = jnp.exp2((s_d - top) * scale).astype(BF16)
+            out = jnp.dot(w_d, vext[rows], preferred_element_type=F32)
+            if i > 0:
+                w_f = jnp.exp2((s_f - top) * scale).astype(BF16)
+                out = out + jnp.dot(w_f, vext[0:i * BQ], preferred_element_type=F32)
+            mbuf[rows, cols] = (out[:, 0:HD] / out[:, HD:]).astype(BF16)
 
     own_tbl.start()
     for k in range(AHEAD):
@@ -308,28 +312,31 @@
     own_tbl.wait()
     q_in.wait()
 
-    events = [functools.partial(ev_own, 0), ev_tables]
-    for r in range(C + 2):
+    def turn(r):
         if r < C:
-            events.append(functools.partial(ev_one, r))
-            if r + 1 < C:
-                events.append(functools.partial(ev_own, r + 1))
+            ev_one(r)
+        if r == 0:
+            ev_tables()
         if 0 <= r - 1 < C:
-            events.append(functools.partial(ev_two, r - 1))
-            events.append(functools.partial(ev_pass1, r - 1))
+            ev_two(r - 1)
+        if r < C:
+            ev_own(r)
+            ev_one_out(r)
+        if 0 <= r - 1 < C:
+            ev_pass1(r - 1)
+            ev_two_out(r - 1)
         if 0 <= r - 2 < C:
-            events.append(functools.partial(ev_far, r - 2))
-    units = NH * NQ
-    at_step = {}
-    for n, e in enumerate(events[:-LATE]):
-        at_step.setdefault(n * units // (len(events) - LATE), []).append(e)
+            ev_far(r - 2)
+
+    units = NH // HG * NQ
+    turns = C + 2
+    early = min(units, turns)
 
     def unit(s, carry):
-        for n, es in at_step.items():
-            @pl.when(s == n)
+        for r in range(early):
+            @pl.when(s == r)
             def _():
-                for e in es:
-                    e()
+                turn(r)
         h, i = s // NQ, s % NQ
         for j in range(NQ):
             @pl.when(i == j)
@@ -340,8 +347,8 @@
     lax.fori_loop(0, units, unit, 0)
     out = pltpu.make_async_copy(mbuf, mixed_hbm, out_sem)
     out.start()
-    for e in events[-LATE:]:
-        e()
+    for r in range(early, turns):
+        turn(r)
     out.wait()
     for k in range(C):
         for d in range(2):
@@ -425,7 +432,7 @@
         in_specs=[anys, anys],
         out_specs=(anys, anys),
         scratch_shapes=[vm(64, PAGE, 2, HD), vm(T, NH * HD), dma(17, 4), dma(2, 4)],
-        compiler_params=pltpu.CompilerParams(vmem_limit_bytes=24 << 20),
+        compiler_params=pltpu.CompilerParams(vmem_limit_bytes=60 << 20),
     )(land.reshape(64, PAGE, 2, HD), mixed)
     return (mixed, store)
 

time: 71.3 us -> 65.4 us (0.917); the launches traced: 71.1 us -> 64.4 us
  Pallas kernels: 66.6 us -> 63.2 us
  local copies, waits for them, and re-layouts: 3.17 us -> 0 us
    pallas_call x1, Pallas kernels: 63.7 us -> 59 us  [on_device(): pl.pallas_call(main_kernel, out_shape=(jax.ShapeDtypeStruct((T, NH * HD),...]
    unnamed x4 -> x0, local copies, waits for them, and re-layouts: 3.17 us -> none
    pallas_call x1, Pallas kernels: 2.94 us -> 4.11 us  [on_device(): pl.pallas_call(layout_kernel, out_shape=(jax.ShapeDtypeStruct((8, PAGE, 2...]
where the time goes in v2:
time: 65.4 us; the launch traced here: 64.4 us
  Pallas kernels  63.2 us (97%)
  between operations  1.29 us (2%)
    pallas_call x1, Pallas kernels, on_device(): pl.pallas_call(main_kernel, out_shape=(jax.ShapeDtypeStruct((T, NH * HD),...  59 us
    pallas_call x1, Pallas kernels, on_device(): pl.pallas_call(layout_kernel, out_shape=(jax.ShapeDtypeStruct((8, PAGE, 2...  4.11 us

profile of v2, /device:TPU:19, one launch (start us, length us, event | category | flops | bytes accessed | tf_op | source)
XLA Modules:
  0.0 64.4 jit_solution(10280965904869743636)
XLA Ops:
  1.3 59.0 %shard_map.77 = (bf16[1024,1024]{1,0:T(8,128)(2,1)}, bf16[64,128,128]{2,1,0:T(8,128)(2,1)}) custom-call(f32[1,128]{1,0:T(1,128)} %constant.2.clone.inv_ref, s32[1]{0:T(128)S(6)} %copy.8.start_ref, s32[16]{0:T(128)} %bitcast.3, bf16[1024,1024]{1,0:T(8,128)(2,1)} %q_hbm.1, bf16[1024,128]{1,0:T(8,128)(2,1)} %k_hbm.1, bf16[1024,128]{1,0:T(8,128)(2,1)} %v_hbm.1), custom_call_target="tpu_custom_call" | custom-call | tf_op jit(solution)/shard_map/pallas_call | solution.py:411
  60.3 4.1 %shard_map.78 = (bf16[8,64,2,1024]{3,2,1,0:T(2,128)(2,1)}, bf16[1024,1024]{1,0:T(8,128)(2,1)}) custom-call(bf16[64,64,2,128]{3,2,1,0:T(2,128)(2,1)} %bitcast.2, bf16[1024,1024]{1,0:T(8,128)(2,1)} %get-tuple-element.7.mixed_in), custom_call_target="tpu_custom_call" | custom-call | tf_op jit(solution)/shard_map/pallas_call | solution.py:429

commit v3 on v2

--- a/solution.py
+++ b/solution.py
@@ -319,8 +319,10 @@
             ev_tables()
         if 0 <= r - 1 < C:
             ev_two(r - 1)
+        if r < C // 2:
+            ev_own(2 * r)
+            ev_own(2 * r + 1)
         if r < C:
-            ev_own(r)
             ev_one_out(r)
         if 0 <= r - 1 < C:
             ev_pass1(r - 1)

time: 65.4 us -> 64.7 us (0.989)
  no operation moved by 1% of the time
where the time goes in v3:
time: 64.7 us; the launch traced here: 63.9 us
  Pallas kernels  62.6 us (97%)
  between operations  1.29 us (2%)
    pallas_call x1, Pallas kernels, on_device(): pl.pallas_call(main_kernel, out_shape=(jax.ShapeDtypeStruct((T, NH * HD),...  58.5 us
    pallas_call x1, Pallas kernels, on_device(): pl.pallas_call(layout_kernel, out_shape=(jax.ShapeDtypeStruct((8, PAGE, 2...  4.11 us

profile of v3, /device:TPU:19, one launch (start us, length us, event | category | flops | bytes accessed | tf_op | source)
XLA Modules:
  0.0 63.9 jit_solution(14439691760305534014)
XLA Ops:
  1.3 58.5 %shard_map.77 = (bf16[1024,1024]{1,0:T(8,128)(2,1)}, bf16[64,128,128]{2,1,0:T(8,128)(2,1)}) custom-call(f32[1,128]{1,0:T(1,128)} %constant.2.clone.inv_ref, s32[1]{0:T(128)S(6)} %copy.8.start_ref, s32[16]{0:T(128)} %bitcast.3, bf16[1024,1024]{1,0:T(8,128)(2,1)} %q_hbm.1, bf16[1024,128]{1,0:T(8,128)(2,1)} %k_hbm.1, bf16[1024,128]{1,0:T(8,128)(2,1)} %v_hbm.1), custom_call_target="tpu_custom_call" | custom-call | tf_op jit(solution)/shard_map/pallas_call | solution.py:413
  59.8 4.1 %shard_map.78 = (bf16[8,64,2,1024]{3,2,1,0:T(2,128)(2,1)}, bf16[1024,1024]{1,0:T(8,128)(2,1)}) custom-call(bf16[64,64,2,128]{3,2,1,0:T(2,128)(2,1)} %bitcast.2, bf16[1024,1024]{1,0:T(8,128)(2,1)} %get-tuple-element.7.mixed_in), custom_call_target="tpu_custom_call" | custom-call | tf_op jit(solution)/shard_map/pallas_call | solution.py:431
